TPU v7x, 512 devices: a whole 4x8x8 slice. The times are simulated.
512 devices in a mesh: ctx: 32 (over z, y_lo), head: 16 (over x, y_hi, core).
Axes of the slice: x: 4, y: 8 (y_hi: 2, y_lo: 4; y = y_hi * 4 + y_lo), z: 8, core: 2. Of those that a mesh axis runs over, the one named last changes fastest.
Arguments:
- ssm_input: bfloat16 [4096, 16384], P('ctx', 'head'), may hold values from -6 to 6
- ssm_gate: bfloat16 [4096, 16384], P('ctx', 'head'), may hold values from -60 to 60
- step_size: float32 [4096, 256], P('ctx', 'head'), may hold values from 0.02 to 0.2
- log_decay: float32 [4096, 256], P('ctx', 'head'), may hold values from -2 to 0
- input_b: bfloat16 [4096, 2048], P('ctx', 'head'), may hold values from -1.796875 to 1.796875
- input_c: bfloat16 [4096, 2048], P('ctx', 'head'), may hold values from -1.796875 to 1.796875
- skip_gain: float32 [256], P('head'), may hold values from 0.5 to 1.5
- norm_gain: float32 [16384], P('head'), may hold values from 0.5 to 1.5
- attn_queries: bfloat16 [4096, 8192], P('ctx', 'head'), may hold values from -30 to 30
- attn_keys: bfloat16 [4096, 1024], P('ctx', 'head'), may hold values from -11 to 11
- attn_values: bfloat16 [4096, 1024], P('ctx', 'head'), may hold values from -6 to 6
Outputs:
- ssm_out: bfloat16 [4096, 16384], P('ctx', 'head')
- attn_out: bfloat16 [4096, 8192], P('ctx', 'head')
All inputs are finite; a program needn't handle non-finite values.
Results may differ from a plain program's by a relative error of at most 0.01.
Values may be sent and summed in bfloat16 or wider, within the bound.
A program may use at most 128 MiB of HBM per device.

v0:
```python
import math

import jax
import jax.numpy as jnp
from jax import lax
from jax.sharding import PartitionSpec as P

P_SIZE = 64
N = 256
HD = 128
SPAN = 128


EPSILON = 1e-05
NEGATIVE = -1e30


def partner(value, axis, distance):
    mask = 2**distance
    pairs = [(source, source ^ mask) for source in range(lax.axis_size(axis))]
    return lax.ppermute(value, axis, pairs)


def entering(array, axis, join, neutral):
    place = lax.axis_index(axis)
    gathered = jax.tree.map(
        lambda a, kind: lax.all_gather(a.astype(kind), axis), array, (jnp.bfloat16, jnp.bfloat16)
    )
    state = jax.tree.map(lambda a, e: jnp.zeros_like(a) + jnp.asarray(e, a.dtype), array, neutral)

    def one(step, state):
        return join(
            state,
            jax.tree.map(
                lambda a, own: lax.dynamic_index_in_dim(a, step, 0, False).astype(own.dtype),
                gathered,
                array,
            ),
        )

    return lax.fori_loop(0, place, one, state)


def pair_join(own_half, other_half):
    is_lower = lax.axis_index("head") % 2 == 0
    return jnp.where(
        is_lower,
        jnp.concatenate([own_half, other_half], axis=-1),
        jnp.concatenate([other_half, own_half], axis=-1),
    )


def chain_combine(earlier, later):
    earlier_log, earlier_state = earlier
    later_log, later_state = later
    return (
        earlier_log + later_log,
        jnp.exp(later_log)[:, None, None] * earlier_state + later_state,
    )


def attend_blocks(carried, pieces, queries, first_query):
    keys_piece, values_piece = pieces
    length = keys_piece.shape[0]
    block_rows = math.gcd(length, 512)
    query_rows = queries.shape[0]
    score_scale = 1.0 / math.sqrt(queries.shape[2])
    query_pos = first_query + jnp.arange(query_rows, dtype=jnp.int32)
    last_query = first_query + query_rows - 1

    def one_block(item_count, running):
        key_first = item_count * block_rows

        def compute(state_in):
            best_score, totals, accumulated = state_in
            key_block = lax.dynamic_slice_in_dim(keys_piece, item_count * block_rows, block_rows, 0)
            value_block = lax.dynamic_slice_in_dim(
                values_piece, item_count * block_rows, block_rows, 0
            )
            scores = (
                jnp.einsum("thd,kd->htk", queries, key_block, preferred_element_type=jnp.float32)
                * score_scale
            )
            key_pos = key_first + jnp.arange(block_rows, dtype=jnp.int32)
            visible = (key_pos[None, :] <= query_pos[:, None])[None]
            scores = jnp.where(visible, scores, NEGATIVE)
            new_best = jnp.maximum(best_score, jnp.max(scores, axis=-1))
            raw_weights = jnp.where(visible, jnp.exp(scores - new_best[..., None]), 0.0)
            factor = jnp.exp(best_score - new_best)
            totals = totals * factor + jnp.sum(raw_weights, axis=-1)
            accumulated = accumulated * factor[..., None] + jnp.einsum(
                "htk,kd->htd",
                raw_weights.astype(jnp.bfloat16),
                value_block,
                preferred_element_type=jnp.float32,
            )
            return (new_best, totals, accumulated)

        return lax.cond(key_first <= last_query, compute, lambda state_in: state_in, running)

    return lax.fori_loop(0, length // block_rows, one_block, carried)


def shards(
    ssm_input,
    ssm_gate,
    step_size,
    log_decay,
    input_b,
    input_c,
    skip_gain,
    norm_gain,
    attn_queries,
    attn_keys,
    attn_values,
):
    local_rows = ssm_input.shape[0]
    head_count = step_size.shape[1]
    query_heads = attn_queries.shape[1] // HD
    ctx_index = lax.axis_index("ctx")
    first_query = ctx_index * local_rows
    queries = attn_queries.reshape(local_rows, query_heads, HD)
    empty_state = (
        jnp.full((query_heads, local_rows), NEGATIVE, jnp.float32),
        jnp.zeros((query_heads, local_rows), jnp.float32),
        jnp.zeros((query_heads, local_rows, HD), jnp.float32),
    )
    other_k, other_v, other_b, other_c = partner(
        (attn_keys, attn_values, input_b, input_c), "head", 0
    )
    full_keys = pair_join(attn_keys, other_k)
    full_values = pair_join(attn_values, other_v)
    full_b = pair_join(input_b, other_b)
    full_c = pair_join(input_c, other_c)
    best_score, totals, accumulated = attend_blocks(
        empty_state,
        (
            lax.all_gather(full_keys, "ctx", axis=0, tiled=True),
            lax.all_gather(full_values, "ctx", axis=0, tiled=True),
        ),
        queries,
        first_query,
    )
    attention = (accumulated / totals[..., None]).astype(jnp.bfloat16)
    attn_out = jnp.transpose(attention, (1, 0, 2)).reshape(local_rows, query_heads * HD)
    block_count = local_rows // SPAN
    inputs_x = ssm_input.reshape(block_count, SPAN, head_count, P_SIZE)
    steps_dt = step_size.reshape(block_count, SPAN, head_count)
    decays = log_decay.reshape(block_count, SPAN, head_count)
    blocks_b = full_b.reshape(block_count, SPAN, N)
    blocks_c = full_c.reshape(block_count, SPAN, N)
    cum_decay = jnp.cumsum(decays, axis=1)
    cum_heads = jnp.swapaxes(cum_decay, 1, 2)
    lower_tri = jnp.arange(SPAN)[:, None] >= jnp.arange(SPAN)[None, :]
    decay_gaps = cum_heads[:, :, :, None] - cum_heads[:, :, None, :]
    decay_mat = jnp.where(lower_tri, jnp.exp(jnp.where(lower_tri, decay_gaps, 0.0)), 0.0)
    inner_cb = jnp.einsum("cqn,ckn->cqk", blocks_c, blocks_b, preferred_element_type=jnp.float32)
    mix_matrix = (
        inner_cb[:, None] * decay_mat * jnp.swapaxes(steps_dt, 1, 2)[:, :, None, :]
    ).astype(jnp.bfloat16)
    within = jnp.einsum("chqk,ckhp->cqhp", mix_matrix, inputs_x, preferred_element_type=jnp.float32)
    weight = jnp.exp(cum_decay[:, -1:, :] - cum_decay) * steps_dt
    weighted_x = inputs_x.astype(jnp.float32) * weight[..., None]
    block_states = jnp.einsum(
        "ckn,ckhp->chnp", blocks_b.astype(jnp.float32), weighted_x, precision=lax.Precision.HIGHEST
    )
    block_ends = jnp.exp(cum_decay[:, -1, :])
    running = jnp.zeros((head_count, N, P_SIZE), jnp.float32)
    entries = [running]
    running = block_ends[0][:, None, None] * running + block_states[0]
    device_log = jnp.sum(decays, axis=(0, 1))
    zero_state = jnp.zeros((head_count, N, P_SIZE), jnp.float32)
    zero_log = jnp.zeros((head_count,), jnp.float32)
    carried_log, incoming = entering(
        (device_log, running), "ctx", chain_combine, (zero_log, zero_state)
    )
    block_logs = cum_decay[:, -1, :]
    enter_decay = jnp.exp(jnp.cumsum(block_logs, axis=0) - block_logs)
    prior = jnp.stack(entries) + enter_decay[:, :, None, None] * incoming[None]
    from_state = jnp.exp(cum_decay)[..., None] * jnp.einsum(
        "cqn,chnp->cqhp", blocks_c.astype(jnp.float32), prior, precision=lax.Precision.HIGHEST
    )
    ssm_y = (
        within + from_state + skip_gain[None, None, :, None] * inputs_x.astype(jnp.float32)
    ).reshape(local_rows, head_count * P_SIZE)
    gated = ssm_y * jax.nn.silu(ssm_gate.astype(jnp.float32))
    own_sum = jnp.sum(gated * gated, axis=-1)
    other_sum = partner(own_sum, "head", 0)
    mean_sq = (own_sum + other_sum) / (2 * gated.shape[1])
    ssm_out = (gated * lax.rsqrt(mean_sq + EPSILON)[:, None] * norm_gain[None, :]).astype(
        jnp.bfloat16
    )
    return (ssm_out, attn_out)


def solution(mesh):
    in_specs = (
        P("ctx", "head"),
        P("ctx", "head"),
        P("ctx", "head"),
        P("ctx", "head"),
        P("ctx", "head"),
        P("ctx", "head"),
        P("head"),
        P("head"),
        P("ctx", "head"),
        P("ctx", "head"),
        P("ctx", "head"),
    )
    out_specs = (P("ctx", "head"), P("ctx", "head"))
    return jax.shard_map(shards, mesh=mesh, in_specs=in_specs, out_specs=out_specs, check_vma=False)
```

profile of v0, /device:TPU:505, one launch (start us, length us, event | category | flops | bytes accessed | tf_op | source)
XLA Modules:
  0.0 839.5 jit_solution(8201528870080409732)
XLA Ops:
  8.2 2.6 collective-permute-start.3
  13.2 2.3 collective-permute-start.4
  17.1 2.3 collective-permute-start.1
  22.3 2.2 fusion.19
  24.6 2.1 collective-permute-start
  30.0 61.9 %all-reduce = bf16[512]{0:T(512)(128)(2,1)S(1)} all-reduce(bf16[512]{0:T(512)(128)(2,1)S(1)} %dynamic-update-slice), channel_id=2, replica_groups=mesh['ctx'=32,'head'=16] {'ctx'}, use_global_device_ids=true, to_apply=%add | all-reduce | flops 512 | bytes 2048
  93.1 49.7 %all-gather.7.cloned.1.call-done = bf16[4096,128]{1,0:T(8,128)(2,1)} async-done(((bf16[128,128]{1,0:T(8,128)(2,1)}), bf16[4096,128]{1,0:T(8,128)(2,1)}) %all-gather.7.cloned.1.call-update) | async-done | bytes 1048592 | tf_op jit(solution)/shard_map/all_gather | solution.py:138
  142.7 154.8 %all-gather.9.cloned.1.call-done = bf16[4096,128]{1,0:T(8,128)(2,1)} async-done(((bf16[128,128]{1,0:T(8,128)(2,1)}), bf16[4096,128]{1,0:T(8,128)(2,1)}) %all-gather.9.cloned.1.call-update) | async-done | bytes 1048592 | tf_op jit(solution)/shard_map/all_gather | solution.py:139
  297.6 24.6 %while.31 = (s32[]{:T(128)}, f32[4,128]{1,0:T(4,128)S(1)}, f32[4,128]{1,0:T(4,128)S(1)}, f32[4,128,128]{2,1,0:T(8,128)S(1)}, s32[]{:T(128)}, /*index=5*/bf16[409...) while((s32[]{:T(128)}, f32[4,128]{1,0:T(4,128)S(1)}, ...), condition=%wide.region_10.11_spmd.clone, body=%wide.region_5.10_spmd.clone.sunk | while | flops 136775296 | bytes 4364621 | solution.py:101
  297.6 3.0 conditional.3
  300.7 3.0 conditional.3
  303.8 3.0 conditional.3
  306.8 3.0 conditional.3
  309.9 3.0 conditional.3
  313.0 3.0 conditional.3
  316.0 3.0 conditional.3
  319.1 3.0 conditional.3
  322.2 370.8 %all-gather.5.cloned.1.call-done = bf16[32,16,256,64]{2,3,1,0:T(8,128)(2,1)} async-done(((bf16[1,16,256,64]{2,3,1,0:T(8,128)(2,1)}), bf16[32,16,256,64]{2,3,1,0:T(8,128)(2,1)}) %all-gather.5.cloned.1.call-update) | async-done | bytes 16777232 | tf_op jit(solution)/shard_map/all_gather | solution.py:27
  693.2 129.8 %while.30 = (s32[]{:T(128)}, f32[16,256,64]{2,1,0:T(8,128)S(1)}, s32[]{:T(128)}, bf16[32,16]{1,0:T(8,128)(2,1)S(1)}, bf16[32,16,256,64]{2,3,1,0:T(8,128)(2,1)}, /*index=5*/s32[]{:T(128)}, s32[]{:T(128)}, s32[]{:T(128)}) while((s32[]{:T(128)}, f32[16,256,64]{2,1,0:T(8,128)S(1)}, s32[]{:T(128)}, bf16[32,16]{1,0:T(8,128)(2,1)S(1)}, ...), condition=%wide.region_3.4_spmd, body=%wide.region_2.3_spmd.sunk | while | flops 786453 | bytes 4718879 | solution.py:41
  693.2 1.9 constant_dynamic-slice_fusion.2
  697.4 1.9 constant_dynamic-slice_fusion.2
  701.6 1.9 constant_dynamic-slice_fusion.2
  705.8 1.9 constant_dynamic-slice_fusion.2
  710.0 1.9 constant_dynamic-slice_fusion.2
  714.2 1.9 constant_dynamic-slice_fusion.2
  718.3 1.9 constant_dynamic-slice_fusion.2
  722.5 1.9 constant_dynamic-slice_fusion.2
  726.7 1.9 constant_dynamic-slice_fusion.2
  776.9 1.9 constant_dynamic-slice_fusion.2
  785.3 1.9 constant_dynamic-slice_fusion.2
  824.6 2.2 copy.82
  828.7 2.6 collective-permute-start.2
  (264 shorter events, 148.3 us)
Async XLA Ops:
  7.2 85.1 %copy-start.10 = (bf16[128,128]{1,0:T(8,128)(2,1)S(1)}, bf16[128,128]{1,0:T(8,128)(2,1)}, u32[]{:S(2)}) copy-start(bf16[128,128]{1,0:T(8,128)(2,1)} %param.21) | copy-start | bytes 98308
  7.2 19.5 %copy-start.7 = (f32[128,16]{0,1:T(8,128)S(1)}, f32[128,16]{0,1:T(8,128)}, u32[]{:S(2)}) copy-start(f32[128,16]{0,1:T(8,128)} %param.20) | copy-start | bytes 24580
  7.2 19.6 %copy-start = (bf16[128,1024]{1,0:T(8,128)(2,1)S(1)}, bf16[128,1024]{1,0:T(8,128)(2,1)}, u32[]{:S(2)}) copy-start(bf16[128,1024]{1,0:T(8,128)(2,1)} %param.17) | copy-start | bytes 786436
  7.2 17.4 %copy-start.6 = (bf16[128,128]{1,0:T(8,128)(2,1)S(1)}, bf16[128,128]{1,0:T(8,128)(2,1)}, u32[]{:S(2)}) copy-start(bf16[128,128]{1,0:T(8,128)(2,1)} %param.22) | copy-start | bytes 98308
  7.2 84.7 %copy-start.5 = (bf16[128,512]{1,0:T(8,128)(2,1)S(1)}, bf16[128,512]{1,0:T(8,128)(2,1)}, u32[]{:S(2)}) copy-start(bf16[128,512]{1,0:T(8,128)(2,1)} %param.25) | copy-start | bytes 393220
  7.2 135.5 %all-gather.7.cloned.1.call-start = ((), (), s32[]{:S(2)}) async-start(), calls=%async_computation.1 | async-start | bytes 1081344 | tf_op jit(solution)/shard_map/all_gather | solution.py:138
  8.2 3.4 collective-permute-start.3
  12.3 285.2 %all-gather.9.cloned.1.call-start = ((), (), s32[]{:S(2)}) async-start(), calls=%async_computation.2 | async-start | bytes 1081344 | tf_op jit(solution)/shard_map/all_gather | solution.py:139
  13.2 3.1 collective-permute-start.4
  17.0 676.0 %all-gather.5.cloned.1.call-start = ((), (), s32[]{:S(2)}) async-start(), calls=%async_computation | async-start | bytes 17301504 | tf_op jit(solution)/shard_map/all_gather | solution.py:27
  17.1 5.2 collective-permute-start.1
  22.3 69.8 %copy-start.3 = (bf16[128,1024]{0,1:T(8,128)(2,1)}, bf16[128,1024]{0,1:T(8,128)(2,1)S(1)}, u32[]{:S(2)}) copy-start(bf16[128,1024]{0,1:T(8,128)(2,1)S(1)} %copy.79) | copy-start | bytes 786436
  24.6 67.7 %collective-permute-start = (bf16[128,128]{1,0:T(8,128)(2,1)S(1)}, bf16[128,128]{1,0:T(8,128)(2,1)S(1)}, u32[]{:S(2)}, u32[]{:S(2)}) collective-permute-start(bf16[128,128]{1,0:T(8,128)(2,1)S(1)} %copy-done.6), channel_id=1, source_target_pairs={{0,1},{1,0},{2,3},{3,2},{4,5},{5,4},{6,7},{7,6},{8,9},{9,8},{10,11... | collective-permute-start | bytes 98312 | tf_op jit(solution)/shard_map/ppermute | solution.py:21
  824.6 2.9 copy-start.2
  824.6 2.9 copy-start.4
  824.6 2.9 copy-start.8
  824.6 2.9 copy-start.11
  824.6 2.9 copy-start.12
  827.5 1.0 copy-start.1
  827.5 4.5 copy-start.9
  828.7 3.4 collective-permute-start.2
Sparse Core Ops, SparseCore 0:
  12.4 130.2 all-gather.6
  144.8 152.6 all-gather.8
  299.6 393.3 all-gather.4
where the time goes:
time: 843 us; the launch traced here: 840 us
  waiting for transfers between devices  577 us (68%)
  local copies, waits for them, and re-layouts  115 us (14%)
  blocking collectives  61.9 us (7%)
  other arithmetic  31.5 us (4%)
  matrix products  24.9 us (3%)
  between operations  14.8 us (2%)
  starting transfers between devices  11.9 us (1%)
    all_gather x1, waiting for transfers between devices, entering(): lax.all_gather(a.astype(kind), axis)  371 us
    all_gather x1, waiting for transfers between devices, shards(): lax.all_gather(full_values, 'ctx', axis=0, tiled=True)  155 us
    dynamic_slice x62, local copies, waits for them, and re-layouts, one(): lax.dynamic_index_in_dim(a, step, 0, False).astype(own.dtype)  106 us
    unnamed x1, blocking collectives  61.9 us
    all_gather x1, waiting for transfers between devices, shards(): lax.all_gather(full_keys, 'ctx', axis=0, tiled=True)  49.7 us
    add x31, other arithmetic, chain_combine(): jnp.exp(later_log)[:, None, None] * earlier_state + later_state  21.9 us
  transfers between devices with their start and end apart: 8, of which 5 were waited for; matrix products, arithmetic and copies ran while one was open for 4% of the time, Pallas kernels for 0%

commit v1 on v0

v1 whole, which is shorter than its diff:
```python
import functools
import math

import jax
import jax.numpy as jnp
from jax import lax
from jax.experimental import pallas as pl
from jax.experimental.pallas import tpu as pltpu
from jax.sharding import PartitionSpec as P

MESH = pl.DeviceIdType.MESH
BF = jnp.bfloat16
F32 = jnp.float32
HI = lax.Precision.HIGHEST

TOK = 128
NZ, NY = 8, 4
HEADS = 16
QW = 256
QH = 4
EPSILON = 1e-05
NEGATIVE = -1e30
SCALE = 1.0 / math.sqrt(128)

NT = (((1,), (1,)), ((), ()))
TN = (((0,), (0,)), ((), ()))


def dot(a, b, dims=(((1,), (0,)), ((), ())), precision=None):
    return lax.dot_general(a, b, dims, precision=precision, preferred_element_type=F32)


def kernel(
    x_hbm, gate_hbm, dt_hbm, ld_hbm, b_hbm, c_hbm, skip_ref, gain_ref, q_hbm, k_hbm, v_hbm,
    ssm_out, attn_out,
    x_ref, gate_ref, dt_ref, ld_ref, q_ref, halves, khalf, vhalf,
    brow, crow, xrow, pk, prow, tb, zin, lam_out, lam_in, rz, rin, early, gout, fs,
    kv, m_ref, l_ref, acc_ref, yb, sq_out, sq_in,
    load_sem, pair_s, pair_r, y_s, y_r, z_s, z_r, kvy_s, kvy_r, kvp_s, kvp_r, kvm_s, kvm_r, kvh_s, kvh_r,
):
    ctx = lax.axis_index("ctx")
    head = lax.axis_index("head")
    z, y = lax.div(ctx, NY), lax.rem(ctx, NY)
    core = lax.rem(head, 2)
    partner = (ctx, head + 1 - 2 * core)
    y_peer = [None] + [(z * NY + lax.rem(y + k, NY), head) for k in range(1, NY)]
    z_peer = [None] + [(lax.rem(z + k, NZ) * NY + y, head) for k in range(1, NZ)]
    y_at = [lax.rem(y + k, NY) for k in range(NY)]
    z_at = [lax.rem(z + k, NZ) for k in range(NZ)]

    barrier = pltpu.get_barrier_semaphore()
    for peer in [partner] + y_peer[1:] + z_peer[1:]:
        pl.semaphore_signal(barrier, inc=1, device_id=peer, device_id_type=MESH)

    loads = [
        pltpu.make_async_copy(src, dst, load_sem.at[i])
        for i, (src, dst) in enumerate(
            [
                (dt_hbm, dt_ref),
                (ld_hbm, ld_ref),
                (k_hbm, khalf.at[core]),
                (v_hbm, vhalf.at[core]),
                (b_hbm, brow.at[y, core]),
                (c_hbm, crow.at[y, core]),
                (x_hbm, x_ref),
                (x_hbm.at[:, pl.ds(pl.multiple_of(y * QW, QW), QW)], xrow.at[y]),
                (q_hbm, q_ref),
                (gate_hbm, gate_ref),
            ]
        )
    ]
    for load in loads:
        load.start()

    sends = []

    def send(src, dst, s_sem, r_sem, device):
        copy = pltpu.make_async_remote_copy(
            src_ref=src, dst_ref=dst, send_sem=s_sem, recv_sem=r_sem, device_id=device, device_id_type=MESH
        )
        copy.start()
        sends.append(copy)
        return copy

    loads[0].wait()
    loads[1].wait()
    row = lax.broadcasted_iota(jnp.int32, (TOK, TOK), 0)
    col = lax.broadcasted_iota(jnp.int32, (TOK, TOK), 1)
    lower = col <= row
    tri = lower.astype(F32)
    eye = (row == col).astype(F32)
    lane = lax.broadcasted_iota(jnp.int32, (1, TOK), 1)
    left = lane < 64
    ld = ld_ref[...]
    cum = dot(tri, ld, precision=HI)
    cum_t = dot(ld, (row <= col).astype(F32), TN, precision=HI)
    dt_t = dot(dt_ref[...], eye, TN, precision=HI)
    block_log = cum_t[:, TOK - 1 : TOK]
    weight_t = jnp.exp(block_log - cum_t) * dt_t
    log_t = jnp.broadcast_to(block_log, (HEADS, TOK))
    for quarter in range(NY):
        heads = slice(4 * quarter, 4 * quarter + 4)
        pk[quarter] = jnp.concatenate([weight_t[heads], log_t[heads]], axis=0)
    prow[y] = pk[y]
    for i in (2, 3, 4, 5):
        loads[i].wait()

    pl.semaphore_wait(barrier, 1 + (NY - 1) + (NZ - 1))

    pair_k = send(khalf.at[core], khalf.at[core], pair_s.at[0], pair_r.at[0], partner)
    pair_v = send(vhalf.at[core], vhalf.at[core], pair_s.at[1], pair_r.at[1], partner)
    pair_b = send(brow.at[y, core], brow.at[y, core], pair_s.at[2], pair_r.at[2], partner)
    pair_c = send(crow.at[y, core], crow.at[y, core], pair_s.at[3], pair_r.at[3], partner)
    y_pk, y_b, y_x, y_c = [None], [None], [None], [None]
    for k in range(1, NY):
        y_b.append(send(brow.at[y, core], brow.at[y, core], y_s.at[0, k], y_r.at[0, k], y_peer[k]))
        y_pk.append(send(pk.at[y_at[k]], prow.at[y], y_s.at[1, k], y_r.at[1, k], y_peer[k]))
    for k in range(1, NY):
        quarter = x_hbm.at[:, pl.ds(pl.multiple_of(y_at[k] * QW, QW), QW)]
        y_x.append(send(quarter, xrow.at[y], y_s.at[2, k], y_r.at[2, k], y_peer[k]))

    pair_k.wait_recv()
    pair_v.wait_recv()
    kv[0, 0, 0] = jnp.concatenate([khalf[0], khalf[1]], axis=1)
    kv[1, 0, 0] = jnp.concatenate([vhalf[0], vhalf[1]], axis=1)

    plus, minus, row_kv, hand = {}, {}, {}, {}

    def send_plus(s, k):
        plus[s, k] = send(
            kv.at[core, s, k], kv.at[core, s + 1, k], kvp_s.at[s, k], kvp_r.at[s, k], z_peer[1]
        )

    def send_minus(s, k):
        minus[s, k] = send(
            kv.at[core, (NZ - s) % NZ, k], kv.at[core, 7 - s, k], kvm_s.at[s, k], kvm_r.at[s, k], z_peer[NZ - 1]
        )

    def hand_over(i, slot, first):
        part = kv.at[core, slot, pl.ds(first, NY - first)]
        hand[slot] = send(part, part, kvh_s.at[i], kvh_r.at[i], partner)

    def pump(s, blocks):
        for k in blocks:
            plus[s, k].wait_recv()
            if s < 3:
                send_plus(s + 1, k)
            if s < 3:
                minus[s, k].wait_recv()
                if s < 2:
                    send_minus(s + 1, k)

    def hand_rows(s):
        hand_over(1 + 2 * s, s + 1, 0)
        if s < 3:
            hand_over(2 + 2 * s, 7 - s, 0)

    send_plus(0, 0)
    send_minus(0, 0)
    for k in range(1, NY):
        row_kv[k] = send(kv.at[core, 0, 0], kv.at[core, 0, NY - k], kvy_s.at[k], kvy_r.at[k], y_peer[k])

    loads[8].wait()

    def attend(keys, values, first=False):
        for h in range(QH):
            scores = dot(q_ref[:, h * 128 : (h + 1) * 128], keys, NT)
            if first:
                scores = jnp.where(lower, scores, NEGATIVE)
                top = jnp.max(scores, axis=1, keepdims=True)
                weights = jnp.exp((scores - top) * SCALE)
                total = jnp.sum(weights, axis=1, keepdims=True)
                mixed = dot(weights.astype(BF), values)
            else:
                before = m_ref[h][:, :1]
                top = jnp.maximum(before, jnp.max(scores, axis=1, keepdims=True))
                factor = jnp.exp((before - top) * SCALE)
                weights = jnp.exp((scores - top) * SCALE)
                total = l_ref[h][:, :1] * factor + jnp.sum(weights, axis=1, keepdims=True)
                mixed = acc_ref[h] * factor + dot(weights.astype(BF), values)
            m_ref[h] = jnp.broadcast_to(top, (TOK, 128))
            l_ref[h] = jnp.broadcast_to(total, (TOK, 128))
            acc_ref[h] = mixed

    def attend_row(slot):
        @pl.when(z >= slot)
        def _():
            attend(kv[0, slot].reshape(NY * TOK, 128), kv[1, slot].reshape(NY * TOK, 128))

    attend(kv[0, 0, 0], kv[1, 0, 0], first=True)

    pair_b.wait_recv()
    pair_c.wait_recv()
    loads[6].wait()
    inner = dot(crow[y, 0], brow[y, 0], NT) + dot(crow[y, 1], brow[y, 1], NT)
    for i in range(HEADS // 2):
        cols = slice(128 * i, 128 * (i + 1))
        x_two = x_ref[:, cols]
        parts = []
        for h in (2 * i, 2 * i + 1):
            gap = jnp.where(lower, cum[:, h : h + 1] - cum_t[h : h + 1, :], NEGATIVE)
            mix = (inner * jnp.exp(gap) * dt_t[h : h + 1, :]).astype(BF)
            parts.append(dot(mix, x_two))
        gain = jnp.where(left, skip_ref[:, 2 * i : 2 * i + 1], skip_ref[:, 2 * i + 1 : 2 * i + 2])
        yb[:, cols] = jnp.where(left, parts[0], parts[1]) + gain * x_two.astype(F32)

    pump(0, [0])

    hand_b = [None]
    for k in range(1, NY):
        y_b[k].wait_recv()
        part = brow.at[y_at[NY - k], core]
        hand_b.append(send(part, part, pair_s.at[3 + k], pair_r.at[3 + k], partner))
    pump(1, [0])
    loads[7].wait()
    for k in range(1, NY):
        y_pk[k].wait_recv()
        y_x[k].wait_recv()
    for k in range(1, NY):
        hand_b[k].wait_recv()
    packed = prow[...]
    columns = packed.reshape(NY * 8, TOK).T

    def two_by_two(parts):
        return jnp.concatenate(
            [jnp.where(left, parts[0], parts[1]), jnp.where(left, parts[2], parts[3])], axis=1
        )

    logs = [two_by_two([packed[j, 4 + i : 5 + i] for i in range(4)]) for j in range(NY)]
    lam_out[...] = jnp.broadcast_to(logs[0] + logs[1] + logs[2] + logs[3], (8, QW))
    z_lam = [None]
    for k in range(1, NZ):
        z_lam.append(send(lam_out, lam_in.at[z], z_s.at[0, k], z_r.at[0, k], z_peer[k]))
    lam_in[z] = lam_out[...]
    state = None
    priors = [None]
    for j in range(NY):
        weight = two_by_two([columns[:, 8 * j + i : 8 * j + i + 1] for i in range(4)])
        weighted = (xrow[j].astype(F32) * weight).astype(BF)
        own = jnp.concatenate([dot(brow[j, 0], weighted, TN), dot(brow[j, 1], weighted, TN)], axis=0)
        state = own if state is None else state * jnp.exp(logs[j]) + own
        priors.append(state)
    tb[...] = state.astype(BF).reshape(NZ, 32, QW)
    z_one = [None]
    for k in range(1, NZ):
        z_one.append(send(tb.at[z_at[k]], zin.at[z], z_s.at[1, k], z_r.at[1, k], z_peer[k]))
    zin[z] = tb[z]
    for k in range(1, NY):
        y_c.append(send(crow.at[y, core], crow.at[y, core], y_s.at[3, k], y_r.at[3, k], y_peer[k]))

    pump(2, [0])
    for k in range(1, NY):
        row_kv[k].wait_recv()
        send_plus(0, NY - k)
        send_minus(0, NY - k)
    hand_over(0, 0, 1)
    pump(3, [0])

    hand_c = [None]
    for k in range(1, NY):
        y_c[k].wait_recv()
        part = crow.at[y_at[NY - k], core]
        hand_c.append(send(part, part, pair_s.at[6 + k], pair_r.at[6 + k], partner))
    for k in range(1, NY):
        hand_c[k].wait_recv()
    for j in range(1, NY):
        prior = priors[j].astype(BF)
        early[j] = dot(crow[j, 0], prior[:128]) + dot(crow[j, 1], prior[128:])

    for k in range(1, NZ):
        z_lam[k].wait_recv()
        z_one[k].wait_recv()
    state = jnp.zeros((32, QW), F32)
    for r in range(NZ):
        rz[r] = state.astype(BF)
        if r < NZ - 1:
            state = state * jnp.exp(lam_in[r, 0:1]) + zin[r].astype(F32)
    z_two = [None]
    for k in range(1, NZ):
        z_two.append(send(rz.at[z_at[k]], rin.at[z], z_s.at[2, k], z_r.at[2, k], z_peer[k]))
    rin[z] = rz[z]

    hand[0].wait_recv()
    for k in range(1, NY):

        @pl.when(y + k >= NY)
        def _():
            attend(kv[0, 0, k], kv[1, 0, k])

    pump(0, [1, 2, 3])
    hand_rows(0)
    pump(1, [1, 2, 3])
    hand_rows(1)
    hand[1].wait_recv()
    attend_row(1)

    for k in range(1, NZ):
        z_two[k].wait_recv()
    entering = rin[...].reshape(QW, QW)
    before = jnp.zeros((1, QW), F32)
    for j in range(NY):
        part = dot(crow[j, 0], entering[:128]) + dot(crow[j, 1], entering[128:])
        if j > 0:
            before = before + logs[j - 1]
            part = part * jnp.exp(before) + early[j]
        gout[j] = part.astype(BF)
    y_out = [None]
    for k in range(1, NY):
        y_out.append(send(gout.at[y_at[k]], fs.at[y], y_s.at[4, k], y_r.at[4, k], y_peer[k]))
    fs[y] = gout[y]

    pump(2, [1, 2, 3])
    hand_rows(2)
    hand[7].wait_recv()
    attend_row(7)
    pump(3, [1, 2, 3])
    hand_rows(3)
    for slot in (2, 6, 3, 5, 4):
        hand[slot].wait_recv()
        attend_row(slot)
    for h in range(QH):
        attn_out[:, h * 128 : (h + 1) * 128] = (acc_ref[h] / l_ref[h]).astype(BF)

    for k in range(1, NY):
        y_out[k].wait_recv()
    loads[9].wait()
    decay = jnp.exp(cum)
    squares = jnp.zeros((TOK, 128), F32)
    for i in range(HEADS // 2):
        cols = slice(128 * i, 128 * (i + 1))
        grow = jnp.where(left, decay[:, 2 * i : 2 * i + 1], decay[:, 2 * i + 1 : 2 * i + 2])
        part = fs[i // 2, :, 128 * (i % 2) : 128 * (i % 2) + 128].astype(F32)
        gate = gate_ref[:, cols].astype(F32)
        gated = (yb[:, cols] + grow * part) * (gate / (1.0 + jnp.exp(-gate)))
        yb[:, cols] = gated
        squares = squares + gated * gated
    own_sum = jnp.sum(squares, axis=1, keepdims=True)
    sq_out[...] = jnp.broadcast_to(own_sum, (TOK, 128))
    send(sq_out, sq_in, pair_s.at[10], pair_r.at[10], partner).wait_recv()
    mean = (sq_out[...] + sq_in[...]) * (1.0 / 2048)
    scale = lax.rsqrt(mean + EPSILON)
    for i in range(HEADS // 2):
        cols = slice(128 * i, 128 * (i + 1))
        ssm_out[:, cols] = (yb[:, cols] * scale * gain_ref[:, cols]).astype(BF)
    for copy in sends:
        copy.wait_send()


def shards(
    ssm_input, ssm_gate, step_size, log_decay, input_b, input_c, skip_gain, norm_gain,
    attn_queries, attn_keys, attn_values,
):
    hbm = pl.BlockSpec(memory_space=pl.ANY)
    vmem = pl.BlockSpec(memory_space=pltpu.VMEM)
    dma = pltpu.SemaphoreType.DMA
    return pl.pallas_call(
        kernel,
        out_shape=(
            jax.ShapeDtypeStruct((TOK, 1024), BF),
            jax.ShapeDtypeStruct((TOK, 512), BF),
        ),
        in_specs=[hbm] * 6 + [vmem] * 2 + [hbm] * 3,
        out_specs=(vmem, vmem),
        scratch_shapes=[
            pltpu.VMEM((TOK, 1024), BF),
            pltpu.VMEM((TOK, 1024), BF),
            pltpu.VMEM((TOK, HEADS), F32),
            pltpu.VMEM((TOK, HEADS), F32),
            pltpu.VMEM((TOK, 512), BF),
            pltpu.VMEM((16, 128), BF),
            pltpu.VMEM((2, TOK, 64), BF),
            pltpu.VMEM((2, TOK, 64), BF),
            pltpu.VMEM((NY, 2, TOK, 128), BF),
            pltpu.VMEM((NY, 2, TOK, 128), BF),
            pltpu.VMEM((NY, TOK, QW), BF),
            pltpu.VMEM((NY, 8, TOK), F32),
            pltpu.VMEM((NY, 8, TOK), F32),
            pltpu.VMEM((NZ, 32, QW), BF),
            pltpu.VMEM((NZ, 32, QW), BF),
            pltpu.VMEM((8, QW), F32),
            pltpu.VMEM((NZ, 8, QW), F32),
            pltpu.VMEM((NZ, 32, QW), BF),
            pltpu.VMEM((NZ, 32, QW), BF),
            pltpu.VMEM((NY, TOK, QW), F32),
            pltpu.VMEM((NY, TOK, QW), BF),
            pltpu.VMEM((NY, TOK, QW), BF),
            pltpu.VMEM((2, NZ, NY, TOK, 128), BF),
            pltpu.VMEM((QH, TOK, 128), F32),
            pltpu.VMEM((QH, TOK, 128), F32),
            pltpu.VMEM((QH, TOK, 128), F32),
            pltpu.VMEM((TOK, 1024), F32),
            pltpu.VMEM((TOK, 128), F32),
            pltpu.VMEM((TOK, 128), F32),
            dma((10,)),
            dma((11,)),
            dma((11,)),
            dma((5, NY)),
            dma((5, NY)),
            dma((3, NZ)),
            dma((3, NZ)),
            dma((NY,)),
            dma((NY,)),
            dma((4, NY)),
            dma((4, NY)),
            dma((3, NY)),
            dma((3, NY)),
            dma((8,)),
            dma((8,)),
        ],
        name="hybrid_mixer",
        compiler_params=pltpu.CompilerParams(
            collective_id=0, has_side_effects=True, vmem_limit_bytes=40 << 20
        ),
    )(
        ssm_input, ssm_gate, step_size, log_decay, input_b, input_c,
        skip_gain.reshape(1, HEADS), norm_gain.reshape(1, 1024),
        attn_queries, attn_keys, attn_values,
    )


def solution(mesh):
    split = P("ctx", "head")
    return jax.shard_map(
        shards,
        mesh=mesh,
        in_specs=(split,) * 6 + (P("head"), P("head")) + (split,) * 3,
        out_specs=(split, split),
        check_vma=False,
    )
```

time: 843 us -> 58.3 us (0.07)
  the two profiles are of different devices: /device:TPU:505 before, /device:TPU:63 now
where the time goes in v1:
time: 58.3 us; the launch traced here: 58 us
  Pallas kernels  50.8 us (87%)
  local copies, waits for them, and re-layouts  6.52 us (11%)
  between operations  0.7 us (1%)
    pallas_call x1, Pallas kernels, shards(): pl.pallas_call(kernel, out_shape=(jax.ShapeDtypeStruct((TOK, 1024), BF),...  50.8 us
    unnamed x22, local copies, waits for them, and re-layouts  6.52 us

profile of v1, /device:TPU:63, one launch (start us, length us, event | category | flops | bytes accessed | tf_op | source)
XLA Modules:
  0.0 58.0 jit_solution(12476093976172139999)
XLA Ops:
  0.6 0.0 copy-start.2
  0.6 0.9 %copy.15.k_hbm = bf16[128,64]{1,0:T(8,128)(2,1)S(1)} copy(bf16[128,64]{0,1:T(8,128)(2,1)} %param.20) | data formatting | bytes 32768 | tf_op args[9]
  1.5 0.8 %copy.16.v_hbm = bf16[128,64]{1,0:T(8,128)(2,1)S(1)} copy(bf16[128,64]{0,1:T(8,128)(2,1)} %param.21) | data formatting | bytes 32768 | tf_op args[10]
  2.3 0.0 copy-start.7
  2.3 0.8 %copy.13.dt_hbm = f32[128,16]{1,0:T(8,128)S(1)} copy(f32[128,16]{0,1:T(8,128)} %param.13) | data formatting | bytes 16384 | tf_op args[2]
  3.2 0.0 copy-done.7
  3.2 0.0 copy-start.3
  3.2 0.0 copy-start.4
  3.2 0.0 copy-start.5
  3.2 0.0 copy-start.6
  3.2 0.1 copy.14.ld_hbm
  3.3 0.0 copy-done.2
  3.3 0.6 %copy-done.3 = bf16[128,128]{1,0:T(8,128)(2,1)S(1)} copy-done((bf16[128,128]{1,0:T(8,128)(2,1)S(1)}, bf16[128,128]{1,0:T(8,128)(2,1)}, u32[]{:S(2)}) %copy-start.3) | copy-done | bytes 32792
  3.9 0.0 copy-done.4
  3.9 0.0 copy-done.5
  3.9 0.0 copy-done.6
  4.0 0.0 copy-start
  4.0 0.9 %copy-done = bf16[128,1024]{1,0:T(8,128)(2,1)S(1)} copy-done((bf16[128,1024]{1,0:T(8,128)(2,1)S(1)}, bf16[128,1024]{1,0:T(8,128)(2,1)}, u32[]{:S(2)}) %copy-start) | copy-done | bytes 262168
  4.9 0.0 copy-start.1
  4.9 0.9 %copy-done.1 = bf16[128,1024]{1,0:T(8,128)(2,1)S(1)} copy-done((bf16[128,1024]{1,0:T(8,128)(2,1)S(1)}, bf16[128,1024]{1,0:T(8,128)(2,1)}, u32[]{:S(2)}) %copy-start.1) | copy-done | bytes 262168
  5.9 50.8 %hybrid_mixer.1 = (bf16[128,1024]{1,0:T(8,128)(2,1)S(1)}, bf16[128,512]{1,0:T(8,128)(2,1)S(1)}) custom-call(bf16[128,1024]{1,0:T(8,128)(2,1)S(1)} %copy-done, bf16[128,1024]{1,0:T(8,128)(2,1)S(1)} %copy-done.1, f32[128,16]{1,0:T(8,128)S(1)} %copy.13.dt_hbm, f32[128,16]{1,0:T(8,128)S(1)} %copy.14.ld_hbm, bf16[128,128]{1,0:T(8,128)(2,1)S(1)} %copy-done.3, ...), custom_call_target="tpu_custom_call" | custom-call | tf_op jit(solution)/shard_map/hybrid_mixer/pallas_call | solution.py:356
  56.6 0.7 %copy.19 = bf16[128,1024]{1,0:T(8,128)(2,1)} copy(bf16[128,1024]{1,0:T(8,128)(2,1)S(1)} %get-tuple-element.4) | data formatting | bytes 524288
  57.3 0.7 %copy.20 = bf16[128,512]{1,0:T(8,128)(2,1)} copy(bf16[128,512]{1,0:T(8,128)(2,1)S(1)} %get-tuple-element.5) | data formatting | bytes 262144
Async XLA Ops:
  0.6 2.7 %copy-start.2 = (bf16[128,512]{1,0:T(8,128)(2,1)S(1)}, bf16[128,512]{1,0:T(8,128)(2,1)}, u32[]{:S(2)}) copy-start(bf16[128,512]{1,0:T(8,128)(2,1)} %q_hbm.1) | copy-start | bytes 393220
  2.3 0.8 %copy-start.7 = (f32[128,16]{0,1:T(8,128)S(1)}, f32[128,16]{0,1:T(8,128)}, u32[]{:S(2)}) copy-start(f32[128,16]{0,1:T(8,128)} %param.14) | copy-start | bytes 24580
  3.2 0.8 %copy-start.3 = (bf16[128,128]{1,0:T(8,128)(2,1)S(1)}, bf16[128,128]{1,0:T(8,128)(2,1)}, u32[]{:S(2)}) copy-start(bf16[128,128]{1,0:T(8,128)(2,1)} %b_hbm.1) | copy-start | bytes 98308
  3.2 0.8 %copy-start.4 = (bf16[128,128]{1,0:T(8,128)(2,1)S(1)}, bf16[128,128]{1,0:T(8,128)(2,1)}, u32[]{:S(2)}) copy-start(bf16[128,128]{1,0:T(8,128)(2,1)} %c_hbm.1) | copy-start | bytes 98308
  3.2 0.8 %copy-start.5 = (f32[1024]{0:T(1024)S(1)}, f32[1024]{0:T(1024)}, u32[]{:S(2)}) copy-start(f32[1024]{0:T(1024)} %param.18) | copy-start | bytes 12292
  3.2 0.7 %copy-start.6 = (f32[16]{0:T(128)S(1)}, f32[16]{0:T(128)}, u32[]{:S(2)}) copy-start(f32[16]{0:T(128)} %param.17) | copy-start | bytes 196
  4.0 1.0 %copy-start = (bf16[128,1024]{1,0:T(8,128)(2,1)S(1)}, bf16[128,1024]{1,0:T(8,128)(2,1)}, u32[]{:S(2)}) copy-start(bf16[128,1024]{1,0:T(8,128)(2,1)} %x_hbm.1) | copy-start | bytes 786436
  4.9 0.9 %copy-start.1 = (bf16[128,1024]{1,0:T(8,128)(2,1)S(1)}, bf16[128,1024]{1,0:T(8,128)(2,1)}, u32[]{:S(2)}) copy-start(bf16[128,1024]{1,0:T(8,128)(2,1)} %gate_hbm.1) | copy-start | bytes 786436

commit v2 on v1

--- a/solution.py
+++ b/solution.py
@@ -33,7 +33,7 @@
 def kernel(
     x_hbm, gate_hbm, dt_hbm, ld_hbm, b_hbm, c_hbm, skip_ref, gain_ref, q_hbm, k_hbm, v_hbm,
     ssm_out, attn_out,
-    x_ref, gate_ref, dt_ref, ld_ref, q_ref, halves, khalf, vhalf,
+    x_ref, gate_ref, dt_ref, ld_ref, q_ref, khalf, vhalf,
     brow, crow, xrow, pk, prow, tb, zin, lam_out, lam_in, rz, rin, early, gout, fs,
     kv, m_ref, l_ref, acc_ref, yb, sq_out, sq_in,
     load_sem, pair_s, pair_r, y_s, y_r, z_s, z_r, kvy_s, kvy_r, kvp_s, kvp_r, kvm_s, kvm_r, kvh_s, kvh_r,
@@ -88,13 +88,12 @@
     col = lax.broadcasted_iota(jnp.int32, (TOK, TOK), 1)
     lower = col <= row
     tri = lower.astype(F32)
-    eye = (row == col).astype(F32)
     lane = lax.broadcasted_iota(jnp.int32, (1, TOK), 1)
     left = lane < 64
-    ld = ld_ref[...]
-    cum = dot(tri, ld, precision=HI)
-    cum_t = dot(ld, (row <= col).astype(F32), TN, precision=HI)
-    dt_t = dot(dt_ref[...], eye, TN, precision=HI)
+    ld_t = ld_ref[...]
+    cum = dot(tri, ld_t, NT, precision=HI)
+    cum_t = dot(ld_t, (row <= col).astype(F32), precision=HI)
+    dt_t = dt_ref[...]
     block_log = cum_t[:, TOK - 1 : TOK]
     weight_t = jnp.exp(block_log - cum_t) * dt_t
     log_t = jnp.broadcast_to(block_log, (HEADS, TOK))
@@ -121,8 +120,8 @@
 
     pair_k.wait_recv()
     pair_v.wait_recv()
-    kv[0, 0, 0] = jnp.concatenate([khalf[0], khalf[1]], axis=1)
-    kv[1, 0, 0] = jnp.concatenate([vhalf[0], vhalf[1]], axis=1)
+    kv[0, 0, 0] = khalf[...].reshape(128, TOK)
+    kv[1, 0, 0] = vhalf[...].reshape(128, TOK).T
 
     plus, minus, row_kv, hand = {}, {}, {}, {}
 
@@ -164,7 +163,8 @@
 
     def attend(keys, values, first=False):
         for h in range(QH):
-            scores = dot(q_ref[:, h * 128 : (h + 1) * 128], keys, NT)
+            query = q_ref[:, h * 128 : (h + 1) * 128]
+            scores = jnp.concatenate([dot(query, part) for part in keys], axis=1)
             if first:
                 scores = jnp.where(lower, scores, NEGATIVE)
                 top = jnp.max(scores, axis=1, keepdims=True)
@@ -185,9 +185,9 @@
     def attend_row(slot):
         @pl.when(z >= slot)
         def _():
-            attend(kv[0, slot].reshape(NY * TOK, 128), kv[1, slot].reshape(NY * TOK, 128))
-
-    attend(kv[0, 0, 0], kv[1, 0, 0], first=True)
+            attend([kv[0, slot, k] for k in range(NY)], kv[1, slot].reshape(NY * TOK, 128))
+
+    attend([kv[0, 0, 0]], kv[1, 0, 0], first=True)
 
     pair_b.wait_recv()
     pair_c.wait_recv()
@@ -285,7 +285,7 @@
 
         @pl.when(y + k >= NY)
         def _():
-            attend(kv[0, 0, k], kv[1, 0, k])
+            attend([kv[0, 0, k]], kv[1, 0, k])
 
     pump(0, [1, 2, 3])
     hand_rows(0)
@@ -350,7 +350,7 @@
     ssm_input, ssm_gate, step_size, log_decay, input_b, input_c, skip_gain, norm_gain,
     attn_queries, attn_keys, attn_values,
 ):
-    hbm = pl.BlockSpec(memory_space=pl.ANY)
+    hbm = pl.BlockSpec(memory_space=pltpu.HBM)
     vmem = pl.BlockSpec(memory_space=pltpu.VMEM)
     dma = pltpu.SemaphoreType.DMA
     return pl.pallas_call(
@@ -364,12 +364,11 @@
         scratch_shapes=[
             pltpu.VMEM((TOK, 1024), BF),
             pltpu.VMEM((TOK, 1024), BF),
-            pltpu.VMEM((TOK, HEADS), F32),
-            pltpu.VMEM((TOK, HEADS), F32),
+            pltpu.VMEM((HEADS, TOK), F32),
+            pltpu.VMEM((HEADS, TOK), F32),
             pltpu.VMEM((TOK, 512), BF),
-            pltpu.VMEM((16, 128), BF),
-            pltpu.VMEM((2, TOK, 64), BF),
-            pltpu.VMEM((2, TOK, 64), BF),
+            pltpu.VMEM((2, 64, TOK), BF),
+            pltpu.VMEM((2, 64, TOK), BF),
             pltpu.VMEM((NY, 2, TOK, 128), BF),
             pltpu.VMEM((NY, 2, TOK, 128), BF),
             pltpu.VMEM((NY, TOK, QW), BF),
@@ -409,12 +408,12 @@
         ],
         name="hybrid_mixer",
         compiler_params=pltpu.CompilerParams(
-            collective_id=0, has_side_effects=True, vmem_limit_bytes=40 << 20
+            collective_id=0, has_side_effects=True, vmem_limit_bytes=56 << 20
         ),
     )(
-        ssm_input, ssm_gate, step_size, log_decay, input_b, input_c,
+        ssm_input, ssm_gate, step_size.T, log_decay.T, input_b, input_c,
         skip_gain.reshape(1, HEADS), norm_gain.reshape(1, 1024),
-        attn_queries, attn_keys, attn_values,
+        attn_queries, attn_keys.T, attn_values.T,
     )
 
 

time: 58.3 us -> 54.8 us (0.940)
  the two profiles are of different devices: /device:TPU:63 before, /device:TPU:125 now
where the time goes in v2:
time: 54.8 us; the launch traced here: 54.6 us
  Pallas kernels  51.5 us (94%)
  local copies, waits for them, and re-layouts  2.36 us (4%)
  between operations  0.65 us (1%)
    pallas_call x1, Pallas kernels, shards(): pl.pallas_call(kernel, out_shape=(jax.ShapeDtypeStruct((TOK, 1024), BF),...  51.5 us
    unnamed x4, local copies, waits for them, and re-layouts  2.36 us

profile of v2, /device:TPU:125, one launch (start us, length us, event | category | flops | bytes accessed | tf_op | source)
XLA Modules:
  0.0 54.6 jit_solution(18093035792824502478)
XLA Ops:
  0.6 51.5 %hybrid_mixer.1 = (bf16[128,1024]{1,0:T(8,128)(2,1)}, bf16[128,512]{1,0:T(8,128)(2,1)}) custom-call(bf16[128,1024]{1,0:T(8,128)(2,1)} %x_hbm.1, bf16[128,1024]{1,0:T(8,128)(2,1)} %gate_hbm.1, f32[16,128]{1,0:T(8,128)} %bitcast.8, f32[16,128]{1,0:T(8,128)} %bitcast.9, bf16[128,128]{1,0:T(8,128)(2,1)} %b_hbm.1, bf16[128,128]{1,0:T(8,128)(2,1)} %c_hbm.1, ...), custom_call_target="tpu_custom_call" | custom-call | tf_op jit(solution)/shard_map/hybrid_mixer/pallas_call | solution.py:356
  52.2 0.0 copy-start
  52.2 1.7 %copy.15 = bf16[128,1024]{1,0:T(8,128)(2,1)} copy(bf16[128,1024]{1,0:T(8,128)(2,1)} %get-tuple-element.4) | data formatting | bytes 524288
  53.9 0.0 copy-done
  53.9 0.7 %copy.16 = bf16[128,512]{1,0:T(8,128)(2,1)} copy(bf16[128,512]{1,0:T(8,128)(2,1)S(1)} %copy-done) | data formatting | bytes 262144
Async XLA Ops:
  52.2 1.7 %copy-start = (bf16[128,512]{1,0:T(8,128)(2,1)S(1)}, bf16[128,512]{1,0:T(8,128)(2,1)}, u32[]{:S(2)}) copy-start(bf16[128,512]{1,0:T(8,128)(2,1)} %get-tuple-element.5) | copy-start | bytes 393220

commit v3 on v2

v3 whole, which is shorter than its diff:
```python
import functools
import math

import jax
import jax.numpy as jnp
from jax import lax
from jax.experimental import pallas as pl
from jax.experimental.pallas import tpu as pltpu
from jax.sharding import PartitionSpec as P

MESH = pl.DeviceIdType.MESH
BF = jnp.bfloat16
F32 = jnp.float32
HI = lax.Precision.HIGHEST

TOK = 128
NZ, NY = 8, 4
HEADS = 16
QW = 256
QH = 4
EPSILON = 1e-05
NEGATIVE = -1e30
SCALE = math.log2(math.e) / math.sqrt(128)

NT = (((1,), (1,)), ((), ()))
TN = (((0,), (0,)), ((), ()))


def dot(a, b, dims=(((1,), (0,)), ((), ())), precision=None):
    return lax.dot_general(a, b, dims, precision=precision, preferred_element_type=F32)


class Transfer:
    def __init__(self, copy, sent=None, received=None):
        self.copy, self.sent, self.received = copy, sent, received

    @staticmethod
    def under(condition, action):
        if condition is None:
            action()
        else:
            pl.when(condition)(lambda: action())

    def start(self):
        self.under(self.sent, self.copy.start)
        return self

    def wait_recv(self):
        self.under(self.received, self.copy.wait_recv)

    def wait_send(self):
        self.under(self.sent, self.copy.wait_send)


def kernel(
    x_hbm, gate_hbm, dt_hbm, ld_hbm, b_hbm, c_hbm, skip_ref, gain_ref, q_hbm, k_hbm, v_hbm,
    ssm_out, attn_out,
    x_ref, gate_ref, dt_ref, ld_ref, q_ref, khalf, vhalf,
    brow, crow, xrow, pk, prow, change, prior, rz, rin, early, gout, fs,
    kv, m_ref, l_ref, acc_ref, stacked, yb, sq_out, sq_in,
    load_sem, pair_s, pair_r, y_s, y_r, z_s, z_r, kvy_s, kvy_r, kvp_s, kvp_r, kvm_s, kvm_r, kvh_s, kvh_r, ready,
):
    ctx = lax.axis_index("ctx")
    head = lax.axis_index("head")
    z, y = lax.div(ctx, NY), lax.rem(ctx, NY)
    core = lax.rem(head, 2)
    partner = (ctx, head + 1 - 2 * core)
    y_peer = [None] + [(z * NY + lax.rem(y + k, NY), head) for k in range(1, NY)]
    next_row = (lax.rem(z + 1, NZ) * NY + y, head)
    last_row = (lax.rem(z + NZ - 1, NZ) * NY + y, head)
    y_at = [lax.rem(y + k, NY) for k in range(NY)]

    barrier = pltpu.get_barrier_semaphore()

    def greet(peer):
        pl.semaphore_signal(barrier, inc=1, device_id=peer, device_id_type=MESH)

    for peer in [partner] + y_peer[1:]:
        greet(peer)
    pl.when(z > 0)(lambda: greet(last_row))
    pl.when(z < NZ - 1)(lambda: greet(next_row))
    for s in (5, 6, 7):

        @pl.when(z + s < NZ)
        def _():
            greet((lax.rem(z + s, NZ) * NY + y, head))


    loads = [
        pltpu.make_async_copy(src, dst, load_sem.at[i])
        for i, (src, dst) in enumerate(
            [
                (dt_hbm, dt_ref),
                (ld_hbm, ld_ref),
                (k_hbm, khalf.at[core]),
                (v_hbm, vhalf.at[core]),
                (b_hbm, brow.at[y, core]),
                (c_hbm, crow.at[y, core]),
                (x_hbm, x_ref),
                (x_hbm.at[:, pl.ds(pl.multiple_of(y * QW, QW), QW)], xrow.at[y]),
                (q_hbm, q_ref),
                (gate_hbm, gate_ref),
            ]
        )
    ]
    for load in loads:
        load.start()

    sends = []

    def plan(src, dst, s_sem, r_sem, device, sent=None, received=None):
        copy = Transfer(
            pltpu.make_async_remote_copy(
                src_ref=src, dst_ref=dst, send_sem=s_sem, recv_sem=r_sem, device_id=device, device_id_type=MESH
            ),
            sent,
            received,
        )
        sends.append(copy)
        return copy

    def send(*args, **kwargs):
        return plan(*args, **kwargs).start()

    y_b, y_pk, y_x, y_c, y_kv, y_out = [None], [None], [None], [None], [None], [None]
    hand_b, hand_c = [None], [None]
    for k in range(1, NY):
        own_b, own_c = brow.at[y, core], crow.at[y, core]
        y_b.append(plan(own_b, own_b, y_s.at[0, k], y_r.at[0, k], y_peer[k]))
        y_pk.append(plan(pk.at[y_at[k]], prow.at[y], y_s.at[1, k], y_r.at[1, k], y_peer[k]))
        quarter = x_hbm.at[:, pl.ds(pl.multiple_of(y_at[k] * QW, QW), QW)]
        y_x.append(plan(quarter, xrow.at[y], y_s.at[2, k], y_r.at[2, k], y_peer[k]))
        y_c.append(plan(own_c, own_c, y_s.at[3, k], y_r.at[3, k], y_peer[k]))
        y_out.append(plan(gout.at[y_at[k]], fs.at[y], y_s.at[4, k], y_r.at[4, k], y_peer[k]))
        y_kv.append(plan(kv.at[core, 0, 0], kv.at[core, 0, NY - k], kvy_s.at[k], kvy_r.at[k], y_peer[k]))
        came_b, came_c = brow.at[y_at[NY - k], core], crow.at[y_at[NY - k], core]
        hand_b.append(plan(came_b, came_b, pair_s.at[3 + k], pair_r.at[3 + k], partner))
        hand_c.append(plan(came_c, came_c, pair_s.at[6 + k], pair_r.at[6 + k], partner))
    plus = {
        (s, k): plan(
            kv.at[core, s, k], kv.at[core, s + 1, k], kvp_s.at[s, k], kvp_r.at[s, k], next_row,
            (z >= s) & (z < NZ - 1), z >= s + 1,
        )
        for s in range(4)
        for k in range(NY)
    }
    far = {
        s: plan(
            kv.at[core, 0], kv.at[core, s], kvm_s.at[s - 5], kvm_r.at[s - 5], (lax.rem(z + s, NZ) * NY + y, head),
            z + s < NZ, z >= s,
        )
        for s in (5, 6, 7)
    }
    hand = []
    for slot in range(NZ):
        part = kv.at[core, slot, pl.ds(1, NY - 1)] if slot == 0 else kv.at[core, slot]
        used = None if slot == 0 else z >= slot
        hand.append(plan(part, part, kvh_s.at[slot], kvh_r.at[slot], partner, used, used))
    z_chain = [
        plan(rz.at[i], rin.at[i], z_s.at[i], z_r.at[i], next_row, z < NZ - 1, z > 0) for i in range(NZ)
    ]
    swap = plan(sq_out, sq_in, pair_s.at[10], pair_r.at[10], partner)

    loads[0].wait()
    loads[1].wait()
    row = lax.broadcasted_iota(jnp.int32, (TOK, TOK), 0)
    col = lax.broadcasted_iota(jnp.int32, (TOK, TOK), 1)
    lower = col <= row
    lane = lax.broadcasted_iota(jnp.int32, (1, TOK), 1)
    left = lane < 64
    ld_t = ld_ref[...]
    cum = dot(lower.astype(F32), ld_t, NT, precision=HI)
    cum_t = dot(ld_t, (row <= col).astype(F32), precision=HI)
    dt_t = dt_ref[...]
    block_log = cum_t[:, TOK - 1 : TOK]
    weight_t = jnp.exp(block_log - cum_t) * dt_t
    log_t = jnp.broadcast_to(block_log, (HEADS, TOK))
    for quarter in range(NY):
        heads = slice(4 * quarter, 4 * quarter + 4)
        pk[quarter] = jnp.concatenate([weight_t[heads], log_t[heads]], axis=0)
    prow[y] = pk[y]
    for i in (2, 3, 4, 5):
        loads[i].wait()
    @pl.when(z == 0)
    def _():
        rin[...] = jnp.zeros_like(rin)

    pl.semaphore_wait(barrier, NY + jnp.where(z > 0, 1, 0) + jnp.where(z < NZ - 1, 1, 0) + jnp.maximum(z - 4, 0))

    for s in (5, 6, 7):

        @pl.when(z >= s)
        def _():
            pl.semaphore_signal(
                ready.at[s - 5], inc=1, device_id=(lax.rem(z + NZ - s, NZ) * NY + y, head), device_id_type=MESH
            )

    pair_k = send(khalf.at[core], khalf.at[core], pair_s.at[0], pair_r.at[0], partner)
    pair_v = send(vhalf.at[core], vhalf.at[core], pair_s.at[1], pair_r.at[1], partner)
    pair_b = send(brow.at[y, core], brow.at[y, core], pair_s.at[2], pair_r.at[2], partner)
    pair_c = send(crow.at[y, core], crow.at[y, core], pair_s.at[3], pair_r.at[3], partner)
    for k in range(1, NY):
        y_b[k].start()
        y_pk[k].start()
    for k in range(1, NY):
        y_x[k].start()

    pair_k.wait_recv()
    pair_v.wait_recv()
    kv[0, 0, 0] = khalf[...].reshape(128, TOK)
    kv[1, 0, 0] = vhalf[...].reshape(128, TOK).T

    def pump(s, blocks):
        for k in blocks:
            plus[s, k].wait_recv()
            if s < 3:
                plus[s + 1, k].start()

    plus[0, 0].start()

    loads[8].wait()

    for h in range(QH):
        stacked[h * TOK : (h + 1) * TOK] = q_ref[:, h * 128 : (h + 1) * 128]

    def attend(keys, values, first=False):
        for h in range(QH):
            rows = slice(h * TOK, (h + 1) * TOK)
            scores = [dot(stacked[rows], part) for part in keys]
            if first:
                scores = [jnp.where(lower, scores[0], NEGATIVE)]
            top = functools.reduce(jnp.maximum, scores)
            top = jnp.broadcast_to(jnp.max(top, axis=1, keepdims=True), (TOK, 128))
            if not first:
                before = m_ref[rows]
                top = jnp.maximum(before, top)
                factor = jnp.exp2((before - top) * SCALE)
            weights = [jnp.exp2((part - top) * SCALE) for part in scores]
            total = functools.reduce(jnp.add, weights)
            mixed = dot(jnp.concatenate([part.astype(BF) for part in weights], axis=1), values)
            m_ref[rows] = top
            l_ref[rows] = total if first else l_ref[rows] * factor + total
            acc_ref[rows] = mixed if first else acc_ref[rows] * factor + mixed

    def attend_row(slot):
        hand[slot].wait_recv()

        @pl.when(z >= slot)
        def _():
            attend([kv[0, slot, k] for k in range(NY)], kv[1, slot].reshape(NY * TOK, 128))

    attend([kv[0, 0, 0]], kv[1, 0, 0], first=True)
    pump(0, [0])

    pair_b.wait_recv()
    pair_c.wait_recv()
    loads[6].wait()
    inner = dot(crow[y, 0], brow[y, 0], NT) + dot(crow[y, 1], brow[y, 1], NT)
    for i in range(HEADS // 2):
        cols = slice(128 * i, 128 * (i + 1))
        x_two = x_ref[:, cols]
        parts = []
        for h in (2 * i, 2 * i + 1):
            gap = jnp.where(lower, cum[:, h : h + 1] - cum_t[h : h + 1, :], NEGATIVE)
            mix = (inner * jnp.exp(gap) * dt_t[h : h + 1, :]).astype(BF)
            parts.append(dot(mix, x_two))
        gain = jnp.where(left, skip_ref[:, 2 * i : 2 * i + 1], skip_ref[:, 2 * i + 1 : 2 * i + 2])
        yb[:, cols] = jnp.where(left, parts[0], parts[1]) + gain * x_two.astype(F32)
        if i == 3:
            pump(1, [0])
    pump(2, [0])

    for k in range(1, NY):
        y_b[k].wait_recv()
        hand_b[k].start()
    loads[7].wait()
    for k in range(1, NY):
        y_pk[k].wait_recv()
        y_x[k].wait_recv()
    for k in range(1, NY):
        y_kv[k].start()
    for k in range(1, NY):
        y_c[k].start()
    for k in range(1, NY):
        hand_b[k].wait_recv()
    packed = prow[...]
    columns = packed.reshape(NY * 8, TOK).T

    def two_by_two(parts):
        return jnp.concatenate(
            [jnp.where(left, parts[0], parts[1]), jnp.where(left, parts[2], parts[3])], axis=1
        )

    logs = [two_by_two([packed[j, 4 + i : 5 + i] for i in range(4)]) for j in range(NY)]
    row_decay = jnp.exp(logs[0] + logs[1] + logs[2] + logs[3])
    state = None
    for j in range(NY):
        weight = two_by_two([columns[:, 8 * j + i : 8 * j + i + 1] for i in range(4)])
        weighted = (xrow[j].astype(F32) * weight).astype(BF)
        own = jnp.concatenate([dot(brow[j, 0], weighted, TN), dot(brow[j, 1], weighted, TN)], axis=0)
        state = own if state is None else state * jnp.exp(logs[j]) + own
        if j < NY - 1:
            prior[j + 1] = state.astype(BF)
    change[...] = state.reshape(NZ, 32, QW)
    pump(3, [0])

    def share_row():
        for k in range(1, NY):
            y_kv[k].wait_recv()
            plus[0, NY - k].start()
        hand[0].start()

        for s in (5, 6, 7):

            @pl.when(z + s < NZ)
            def _():
                pl.semaphore_wait(ready.at[s - 5], 1)

            far[s].start()


    def row_part():
        for k in range(1, NY):
            y_c[k].wait_recv()
            hand_c[k].start()
        for k in range(1, NY):
            hand_c[k].wait_recv()
        for j in range(1, NY):
            early[j] = dot(crow[j, 0], prior[j, :128]) + dot(crow[j, 1], prior[j, 128:])

    def near_rows():
        pump(0, [1, 2, 3])
        hand[1].start()
        hand[0].wait_recv()
        for k in range(1, NY):

            @pl.when(y + k >= NY)
            def _():
                attend([kv[0, 0, k]], kv[1, 0, k])

        pump(1, [1, 2, 3])
        hand[2].start()
        attend_row(1)

    late = z >= 7

    @pl.when(z >= 4)
    def _():
        share_row()
        row_part()

    pl.when(late)(near_rows)
    for i in range(NZ):
        z_chain[i].wait_recv()
        rz[i] = (rin[i].astype(F32) * row_decay + change[i]).astype(BF)
        z_chain[i].start()

    @pl.when(z < 4)
    def _():
        share_row()
        row_part()

    entering = rin[...].reshape(QW, QW)
    before = jnp.zeros((1, QW), F32)
    for j in range(NY):
        part = dot(crow[j, 0], entering[:128]) + dot(crow[j, 1], entering[128:])
        if j > 0:
            before = before + logs[j - 1]
            part = part * jnp.exp(before) + early[j]
        gout[j] = part.astype(BF)
    for k in range(1, NY):
        y_out[k].start()
    fs[y] = gout[y]

    pl.when(~late)(near_rows)
    pump(2, [1, 2, 3])
    hand[3].start()
    attend_row(2)
    pump(3, [1, 2, 3])
    hand[4].start()
    for slot in (7, 6, 5):
        far[slot].wait_recv()
        hand[slot].start()
    for slot in (3, 4, 7, 6, 5):
        attend_row(slot)
    for h in range(QH):
        rows = slice(h * TOK, (h + 1) * TOK)
        attn_out[:, h * 128 : (h + 1) * 128] = (acc_ref[rows] / jnp.sum(l_ref[rows], axis=1, keepdims=True)).astype(BF)

    for k in range(1, NY):
        y_out[k].wait_recv()
    loads[9].wait()
    decay = jnp.exp(cum)
    squares = jnp.zeros((TOK, 128), F32)
    for i in range(HEADS // 2):
        cols = slice(128 * i, 128 * (i + 1))
        grow = jnp.where(left, decay[:, 2 * i : 2 * i + 1], decay[:, 2 * i + 1 : 2 * i + 2])
        part = fs[i // 2, :, 128 * (i % 2) : 128 * (i % 2) + 128].astype(F32)
        gate = gate_ref[:, cols].astype(F32)
        gated = (yb[:, cols] + grow * part) * (gate / (1.0 + jnp.exp(-gate)))
        yb[:, cols] = gated
        squares = squares + gated * gated
    own_sum = jnp.sum(squares, axis=1, keepdims=True)
    sq_out[...] = jnp.broadcast_to(own_sum, (TOK, 128))
    swap.start()
    swap.wait_recv()
    mean = (sq_out[...] + sq_in[...]) * (1.0 / 2048)
    scale = lax.rsqrt(mean + EPSILON)
    for i in range(HEADS // 2):
        cols = slice(128 * i, 128 * (i + 1))
        ssm_out[:, cols] = (yb[:, cols] * scale * gain_ref[:, cols]).astype(BF)
    for copy in sends:
        copy.wait_send()


def shards(
    ssm_input, ssm_gate, step_size, log_decay, input_b, input_c, skip_gain, norm_gain,
    attn_queries, attn_keys, attn_values,
):
    hbm = pl.BlockSpec(memory_space=pltpu.HBM)
    vmem = pl.BlockSpec(memory_space=pltpu.VMEM)
    dma = pltpu.SemaphoreType.DMA
    return pl.pallas_call(
        kernel,
        out_shape=(
            jax.ShapeDtypeStruct((TOK, 1024), BF),
            jax.ShapeDtypeStruct((TOK, 512), BF),
        ),
        in_specs=[hbm] * 6 + [vmem] * 2 + [hbm] * 3,
        out_specs=(vmem, vmem),
        scratch_shapes=[
            pltpu.VMEM((TOK, 1024), BF),
            pltpu.VMEM((TOK, 1024), BF),
            pltpu.VMEM((HEADS, TOK), F32),
            pltpu.VMEM((HEADS, TOK), F32),
            pltpu.VMEM((TOK, 512), BF),
            pltpu.VMEM((2, 64, TOK), BF),
            pltpu.VMEM((2, 64, TOK), BF),
            pltpu.VMEM((NY, 2, TOK, 128), BF),
            pltpu.VMEM((NY, 2, TOK, 128), BF),
            pltpu.VMEM((NY, TOK, QW), BF),
            pltpu.VMEM((NY, 8, TOK), F32),
            pltpu.VMEM((NY, 8, TOK), F32),
            pltpu.VMEM((NZ, 32, QW), F32),
            pltpu.VMEM((NY, QW, QW), BF),
            pltpu.VMEM((NZ, 32, QW), BF),
            pltpu.VMEM((NZ, 32, QW), BF),
            pltpu.VMEM((NY, TOK, QW), F32),
            pltpu.VMEM((NY, TOK, QW), BF),
            pltpu.VMEM((NY, TOK, QW), BF),
            pltpu.VMEM((2, NZ, NY, TOK, 128), BF),
            pltpu.VMEM((QH * TOK, 128), F32),
            pltpu.VMEM((QH * TOK, 128), F32),
            pltpu.VMEM((QH * TOK, 128), F32),
            pltpu.VMEM((QH * TOK, 128), BF),
            pltpu.VMEM((TOK, 1024), F32),
            pltpu.VMEM((TOK, 128), F32),
            pltpu.VMEM((TOK, 128), F32),
            dma((10,)),
            dma((11,)),
            dma((11,)),
            dma((5, NY)),
            dma((5, NY)),
            dma((NZ,)),
            dma((NZ,)),
            dma((NY,)),
            dma((NY,)),
            dma((4, NY)),
            dma((4, NY)),
            dma((3,)),
            dma((3,)),
            dma((8,)),
            dma((8,)),
            pltpu.SemaphoreType.REGULAR((3,)),
        ],
        name="hybrid_mixer",
        compiler_params=pltpu.CompilerParams(
            collective_id=0, has_side_effects=True, vmem_limit_bytes=56 << 20
        ),
    )(
        ssm_input, ssm_gate, step_size.T, log_decay.T, input_b, input_c,
        skip_gain.reshape(1, HEADS), norm_gain.reshape(1, 1024),
        attn_queries, attn_keys.T, attn_values.T,
    )


def solution(mesh):
    split = P("ctx", "head")
    return jax.shard_map(
        shards,
        mesh=mesh,
        in_specs=(split,) * 6 + (P("head"), P("head")) + (split,) * 3,
        out_specs=(split, split),
        check_vma=False,
    )
```

time: 54.8 us -> 51.5 us (0.940)
  the two profiles are of different devices: /device:TPU:125 before, /device:TPU:505 now
where the time goes in v3:
time: 51.5 us; the launch traced here: 50.5 us
  Pallas kernels  47.5 us (92%)
  local copies, waits for them, and re-layouts  2.36 us (5%)
  between operations  0.65 us (1%)
    pallas_call x1, Pallas kernels, shards(): pl.pallas_call(kernel, out_shape=(jax.ShapeDtypeStruct((TOK, 1024), BF),...  47.5 us
    unnamed x4, local copies, waits for them, and re-layouts  2.36 us

profile of v3, /device:TPU:505, one launch (start us, length us, event | category | flops | bytes accessed | tf_op | source)
XLA Modules:
  0.0 50.5 jit_solution(3992934791168286222)
XLA Ops:
  0.6 47.5 %hybrid_mixer.1 = (bf16[128,1024]{1,0:T(8,128)(2,1)}, bf16[128,512]{1,0:T(8,128)(2,1)}) custom-call(bf16[128,1024]{1,0:T(8,128)(2,1)} %x_hbm.1, bf16[128,1024]{1,0:T(8,128)(2,1)} %gate_hbm.1, f32[16,128]{1,0:T(8,128)} %bitcast.8, f32[16,128]{1,0:T(8,128)} %bitcast.9, bf16[128,128]{1,0:T(8,128)(2,1)} %b_hbm.1, bf16[128,128]{1,0:T(8,128)(2,1)} %c_hbm.1, ...), custom_call_target="tpu_custom_call" | custom-call | tf_op jit(solution)/shard_map/hybrid_mixer/pallas_call | solution.py:423
  48.1 0.0 copy-start
  48.1 1.7 %copy.15 = bf16[128,1024]{1,0:T(8,128)(2,1)} copy(bf16[128,1024]{1,0:T(8,128)(2,1)} %get-tuple-element.4) | data formatting | bytes 524288
  49.9 0.0 copy-done
  49.9 0.7 %copy.16 = bf16[128,512]{1,0:T(8,128)(2,1)} copy(bf16[128,512]{1,0:T(8,128)(2,1)S(1)} %copy-done) | data formatting | bytes 262144
Async XLA Ops:
  48.1 1.7 %copy-start = (bf16[128,512]{1,0:T(8,128)(2,1)S(1)}, bf16[128,512]{1,0:T(8,128)(2,1)}, u32[]{:S(2)}) copy-start(bf16[128,512]{1,0:T(8,128)(2,1)} %get-tuple-element.5) | copy-start | bytes 393220

commit v4 on v3

--- a/solution.py
+++ b/solution.py
@@ -57,7 +57,7 @@
     ssm_out, attn_out,
     x_ref, gate_ref, dt_ref, ld_ref, q_ref, khalf, vhalf,
     brow, crow, xrow, pk, prow, change, prior, rz, rin, early, gout, fs,
-    kv, m_ref, l_ref, acc_ref, stacked, yb, sq_out, sq_in,
+    kv, m_ref, l_ref, acc_ref, stacked, yb, open_gate, sq_out, sq_in,
     load_sem, pair_s, pair_r, y_s, y_r, z_s, z_r, kvy_s, kvy_r, kvp_s, kvp_r, kvm_s, kvm_r, kvh_s, kvh_r, ready,
 ):
     ctx = lax.axis_index("ctx")
@@ -122,7 +122,7 @@
     def send(*args, **kwargs):
         return plan(*args, **kwargs).start()
 
-    y_b, y_pk, y_x, y_c, y_kv, y_out = [None], [None], [None], [None], [None], [None]
+    y_b, y_pk, y_x, y_c, y_kv = [None], [None], [None], [None], [None]
     hand_b, hand_c = [None], [None]
     for k in range(1, NY):
         own_b, own_c = brow.at[y, core], crow.at[y, core]
@@ -131,7 +131,6 @@
         quarter = x_hbm.at[:, pl.ds(pl.multiple_of(y_at[k] * QW, QW), QW)]
         y_x.append(plan(quarter, xrow.at[y], y_s.at[2, k], y_r.at[2, k], y_peer[k]))
         y_c.append(plan(own_c, own_c, y_s.at[3, k], y_r.at[3, k], y_peer[k]))
-        y_out.append(plan(gout.at[y_at[k]], fs.at[y], y_s.at[4, k], y_r.at[4, k], y_peer[k]))
         y_kv.append(plan(kv.at[core, 0, 0], kv.at[core, 0, NY - k], kvy_s.at[k], kvy_r.at[k], y_peer[k]))
         came_b, came_c = brow.at[y_at[NY - k], core], crow.at[y_at[NY - k], core]
         hand_b.append(plan(came_b, came_b, pair_s.at[3 + k], pair_r.at[3 + k], partner))
@@ -153,11 +152,29 @@
     }
     hand = []
     for slot in range(NZ):
-        part = kv.at[core, slot, pl.ds(1, NY - 1)] if slot == 0 else kv.at[core, slot]
+        part = kv.at[core, slot, pl.ds(1, NY - 1)] if slot < 5 else kv.at[core, slot]
         used = None if slot == 0 else z >= slot
         hand.append(plan(part, part, kvh_s.at[slot], kvh_r.at[slot], partner, used, used))
+    hand_own = [None]
+    for slot in range(1, 5):
+        part = kv.at[core, slot, 0]
+        hand_own.append(plan(part, part, kvh_s.at[7 + slot], kvh_r.at[7 + slot], partner, z >= slot, z >= slot))
     z_chain = [
         plan(rz.at[i], rin.at[i], z_s.at[i], z_r.at[i], next_row, z < NZ - 1, z > 0) for i in range(NZ)
+    ]
+    y_out = [
+        plan(gout.at[j], fs.at[y], y_s.at[4, j], y_r.at[4, y], (z * NY + j, head), y != j) for j in range(NY)
+    ]
+    y_in = [
+        Transfer(
+            pltpu.make_async_remote_copy(
+                src_ref=gout.at[j], dst_ref=fs.at[j], send_sem=y_s.at[4, j], recv_sem=y_r.at[4, j],
+                device_id=(z * NY + j, head), device_id_type=MESH,
+            ),
+            None,
+            y != j,
+        )
+        for j in range(NY)
     ]
     swap = plan(sq_out, sq_in, pair_s.at[10], pair_r.at[10], partner)
 
@@ -242,19 +259,36 @@
             l_ref[rows] = total if first else l_ref[rows] * factor + total
             acc_ref[rows] = mixed if first else acc_ref[rows] * factor + mixed
 
+    late = z >= 5
+
     def attend_row(slot):
         hand[slot].wait_recv()
 
-        @pl.when(z >= slot)
+        @pl.when((z >= slot) & (~late if slot < 5 else late))
         def _():
             attend([kv[0, slot, k] for k in range(NY)], kv[1, slot].reshape(NY * TOK, 128))
 
+        if slot < 5:
+
+            @pl.when(late)
+            def _():
+                attend([kv[0, slot, k] for k in range(1, NY)], kv[1, slot, 1:].reshape((NY - 1) * TOK, 128))
+
+    def attend_column():
+        attend(
+            [kv[0, slot, 0] for slot in range(1, 5)],
+            jnp.concatenate([kv[1, slot, 0] for slot in range(1, 5)], axis=0),
+        )
+
     attend([kv[0, 0, 0]], kv[1, 0, 0], first=True)
     pump(0, [0])
+    hand_own[1].start()
 
     pair_b.wait_recv()
     pair_c.wait_recv()
     loads[6].wait()
+    loads[9].wait()
+    decay = jnp.exp(cum)
     inner = dot(crow[y, 0], brow[y, 0], NT) + dot(crow[y, 1], brow[y, 1], NT)
     for i in range(HEADS // 2):
         cols = slice(128 * i, 128 * (i + 1))
@@ -265,10 +299,16 @@
             mix = (inner * jnp.exp(gap) * dt_t[h : h + 1, :]).astype(BF)
             parts.append(dot(mix, x_two))
         gain = jnp.where(left, skip_ref[:, 2 * i : 2 * i + 1], skip_ref[:, 2 * i + 1 : 2 * i + 2])
-        yb[:, cols] = jnp.where(left, parts[0], parts[1]) + gain * x_two.astype(F32)
+        gate = gate_ref[:, cols].astype(F32)
+        gate = gate / (1.0 + jnp.exp(-gate))
+        grow = jnp.where(left, decay[:, 2 * i : 2 * i + 1], decay[:, 2 * i + 1 : 2 * i + 2])
+        yb[:, cols] = (jnp.where(left, parts[0], parts[1]) + gain * x_two.astype(F32)) * gate
+        open_gate[:, cols] = gate * grow
         if i == 3:
             pump(1, [0])
+            hand_own[2].start()
     pump(2, [0])
+    hand_own[3].start()
 
     for k in range(1, NY):
         y_b[k].wait_recv()
@@ -303,6 +343,7 @@
             prior[j + 1] = state.astype(BF)
     change[...] = state.reshape(NZ, 32, QW)
     pump(3, [0])
+    hand_own[4].start()
 
     def share_row():
         for k in range(1, NY):
@@ -317,7 +358,6 @@
                 pl.semaphore_wait(ready.at[s - 5], 1)
 
             far[s].start()
-
 
     def row_part():
         for k in range(1, NY):
@@ -328,9 +368,7 @@
         for j in range(1, NY):
             early[j] = dot(crow[j, 0], prior[j, :128]) + dot(crow[j, 1], prior[j, 128:])
 
-    def near_rows():
-        pump(0, [1, 2, 3])
-        hand[1].start()
+    def attend_own():
         hand[0].wait_recv()
         for k in range(1, NY):
 
@@ -338,18 +376,16 @@
             def _():
                 attend([kv[0, 0, k]], kv[1, 0, k])
 
-        pump(1, [1, 2, 3])
-        hand[2].start()
-        attend_row(1)
-
-    late = z >= 7
 
     @pl.when(z >= 4)
     def _():
         share_row()
         row_part()
 
-    pl.when(late)(near_rows)
+    for copy in hand_own[1:]:
+        copy.wait_recv()
+    pl.when(late)(attend_column)
+    pl.when(late)(attend_own)
     for i in range(NZ):
         z_chain[i].wait_recv()
         rz[i] = (rin[i].astype(F32) * row_decay + change[i]).astype(BF)
@@ -368,36 +404,39 @@
             before = before + logs[j - 1]
             part = part * jnp.exp(before) + early[j]
         gout[j] = part.astype(BF)
-    for k in range(1, NY):
-        y_out[k].start()
+        y_out[j].start()
     fs[y] = gout[y]
 
-    pl.when(~late)(near_rows)
-    pump(2, [1, 2, 3])
-    hand[3].start()
-    attend_row(2)
-    pump(3, [1, 2, 3])
-    hand[4].start()
+    pump(0, [1, 2, 3])
+    hand[1].start()
+    pl.when(~late)(attend_own)
+    pump(1, [1, 2, 3])
+    hand[2].start()
+    attend_row(1)
     for slot in (7, 6, 5):
         far[slot].wait_recv()
         hand[slot].start()
-    for slot in (3, 4, 7, 6, 5):
-        attend_row(slot)
+    attend_row(2)
+    attend_row(7)
+    attend_row(6)
+    pump(2, [1, 2, 3])
+    hand[3].start()
+    attend_row(5)
+    pump(3, [1, 2, 3])
+    hand[4].start()
+    attend_row(3)
+    attend_row(4)
     for h in range(QH):
         rows = slice(h * TOK, (h + 1) * TOK)
         attn_out[:, h * 128 : (h + 1) * 128] = (acc_ref[rows] / jnp.sum(l_ref[rows], axis=1, keepdims=True)).astype(BF)
 
-    for k in range(1, NY):
-        y_out[k].wait_recv()
-    loads[9].wait()
-    decay = jnp.exp(cum)
+    for copy in y_in:
+        copy.wait_recv()
     squares = jnp.zeros((TOK, 128), F32)
     for i in range(HEADS // 2):
         cols = slice(128 * i, 128 * (i + 1))
-        grow = jnp.where(left, decay[:, 2 * i : 2 * i + 1], decay[:, 2 * i + 1 : 2 * i + 2])
         part = fs[i // 2, :, 128 * (i % 2) : 128 * (i % 2) + 128].astype(F32)
-        gate = gate_ref[:, cols].astype(F32)
-        gated = (yb[:, cols] + grow * part) * (gate / (1.0 + jnp.exp(-gate)))
+        gated = yb[:, cols] + open_gate[:, cols] * part
         yb[:, cols] = gated
         squares = squares + gated * gated
     own_sum = jnp.sum(squares, axis=1, keepdims=True)
@@ -454,6 +493,7 @@
             pltpu.VMEM((QH * TOK, 128), F32),
             pltpu.VMEM((QH * TOK, 128), BF),
             pltpu.VMEM((TOK, 1024), F32),
+            pltpu.VMEM((TOK, 1024), F32),
             pltpu.VMEM((TOK, 128), F32),
             pltpu.VMEM((TOK, 128), F32),
             dma((10,)),
@@ -469,8 +509,8 @@
             dma((4, NY)),
             dma((3,)),
             dma((3,)),
-            dma((8,)),
-            dma((8,)),
+            dma((12,)),
+            dma((12,)),
             pltpu.SemaphoreType.REGULAR((3,)),
         ],
         name="hybrid_mixer",

time: 51.5 us -> 50.3 us (0.977)
  Pallas kernels: 47.5 us -> 46.8 us
    pallas_call x1, Pallas kernels: 47.5 us -> 46.8 us  [shards(): pl.pallas_call(kernel, out_shape=(jax.ShapeDtypeStruct((TOK, 1024), BF),...]
where the time goes in v4:
time: 50.3 us; the launch traced here: 49.8 us
  Pallas kernels  46.8 us (93%)
  local copies, waits for them, and re-layouts  2.36 us (5%)
  between operations  0.65 us (1%)
    pallas_call x1, Pallas kernels, shards(): pl.pallas_call(kernel, out_shape=(jax.ShapeDtypeStruct((TOK, 1024), BF),...  46.8 us
    unnamed x4, local copies, waits for them, and re-layouts  2.36 us

profile of v4, /device:TPU:505, one launch (start us, length us, event | category | flops | bytes accessed | tf_op | source)
XLA Modules:
  0.0 49.8 jit_solution(17191413794599957318)
XLA Ops:
  0.6 46.8 %hybrid_mixer.1 = (bf16[128,1024]{1,0:T(8,128)(2,1)}, bf16[128,512]{1,0:T(8,128)(2,1)}) custom-call(bf16[128,1024]{1,0:T(8,128)(2,1)} %x_hbm.1, bf16[128,1024]{1,0:T(8,128)(2,1)} %gate_hbm.1, f32[16,128]{1,0:T(8,128)} %bitcast.8, f32[16,128]{1,0:T(8,128)} %bitcast.9, bf16[128,128]{1,0:T(8,128)(2,1)} %b_hbm.1, bf16[128,128]{1,0:T(8,128)(2,1)} %c_hbm.1, ...), custom_call_target="tpu_custom_call" | custom-call | tf_op jit(solution)/shard_map/hybrid_mixer/pallas_call | solution.py:462
  47.4 0.0 copy-start
  47.4 1.7 %copy.15 = bf16[128,1024]{1,0:T(8,128)(2,1)} copy(bf16[128,1024]{1,0:T(8,128)(2,1)} %get-tuple-element.4) | data formatting | bytes 524288
  49.2 0.0 copy-done
  49.2 0.7 %copy.16 = bf16[128,512]{1,0:T(8,128)(2,1)} copy(bf16[128,512]{1,0:T(8,128)(2,1)S(1)} %copy-done) | data formatting | bytes 262144
Async XLA Ops:
  47.4 1.7 %copy-start = (bf16[128,512]{1,0:T(8,128)(2,1)S(1)}, bf16[128,512]{1,0:T(8,128)(2,1)}, u32[]{:S(2)}) copy-start(bf16[128,512]{1,0:T(8,128)(2,1)} %get-tuple-element.5) | copy-start | bytes 393220

commit v5 on v4

--- a/solution.py
+++ b/solution.py
@@ -452,6 +452,11 @@
         copy.wait_send()
 
 
+def hand_out(ssm, attention, ssm_out, attn_out):
+    ssm_out[...] = ssm[...]
+    attn_out[...] = attention[...]
+
+
 def shards(
     ssm_input, ssm_gate, step_size, log_decay, input_b, input_c, skip_gain, norm_gain,
     attn_queries, attn_keys, attn_values,
@@ -459,7 +464,7 @@
     hbm = pl.BlockSpec(memory_space=pltpu.HBM)
     vmem = pl.BlockSpec(memory_space=pltpu.VMEM)
     dma = pltpu.SemaphoreType.DMA
-    return pl.pallas_call(
+    ssm, attention = pl.pallas_call(
         kernel,
         out_shape=(
             jax.ShapeDtypeStruct((TOK, 1024), BF),
@@ -522,6 +527,16 @@
         skip_gain.reshape(1, HEADS), norm_gain.reshape(1, 1024),
         attn_queries, attn_keys.T, attn_values.T,
     )
+    return pl.pallas_call(
+        hand_out,
+        out_shape=(
+            jax.ShapeDtypeStruct((TOK, 1024), BF),
+            jax.ShapeDtypeStruct((TOK, 512), BF),
+        ),
+        in_specs=[vmem] * 2,
+        out_specs=(vmem, vmem),
+        name="hand_out",
+    )(ssm, attention)
 
 
 def solution(mesh):

time: 50.3 us -> 49.7 us (0.988)
  local copies, waits for them, and re-layouts: 2.36 us -> 0 us
  Pallas kernels: 46.8 us -> 48.5 us
    unnamed x4 -> x0, local copies, waits for them, and re-layouts: 2.36 us -> none
    pallas_call x0 -> x1, Pallas kernels: none -> 1.74 us  [shards(): pl.pallas_call(hand_out, out_shape=(jax.ShapeDtypeStruct((TOK, 1024), BF)...]
where the time goes in v5:
time: 49.7 us; the launch traced here: 49.2 us
  Pallas kernels  48.5 us (98%)
  between operations  0.64 us (1%)
    pallas_call x1, Pallas kernels, shards(): pl.pallas_call(kernel, out_shape=(jax.ShapeDtypeStruct((TOK, 1024), BF),...  46.8 us
    pallas_call x1, Pallas kernels, shards(): pl.pallas_call(hand_out, out_shape=(jax.ShapeDtypeStruct((TOK, 1024), BF)...  1.74 us

profile of v5, /device:TPU:505, one launch (start us, length us, event | category | flops | bytes accessed | tf_op | source)
XLA Modules:
  0.0 49.2 jit_solution(4861452207034918845)
XLA Ops:
  0.6 46.8 %hybrid_mixer.1 = (bf16[128,1024]{1,0:T(8,128)(2,1)}, bf16[128,512]{1,0:T(8,128)(2,1)}) custom-call(bf16[128,1024]{1,0:T(8,128)(2,1)} %x_hbm.1, bf16[128,1024]{1,0:T(8,128)(2,1)} %gate_hbm.1, f32[16,128]{1,0:T(8,128)} %bitcast.8, f32[16,128]{1,0:T(8,128)} %bitcast.9, bf16[128,128]{1,0:T(8,128)(2,1)} %b_hbm.1, bf16[128,128]{1,0:T(8,128)(2,1)} %c_hbm.1, ...), custom_call_target="tpu_custom_call" | custom-call | tf_op jit(solution)/shard_map/hybrid_mixer/pallas_call | solution.py:467
  47.4 1.7 %hand_out.1 = (bf16[128,1024]{1,0:T(8,128)(2,1)}, bf16[128,512]{1,0:T(8,128)(2,1)}) custom-call(bf16[128,1024]{1,0:T(8,128)(2,1)} %get-tuple-element.4.ssm, bf16[128,512]{1,0:T(8,128)(2,1)} %get-tuple-element.5.attention), custom_call_target="tpu_custom_call" | custom-call | tf_op jit(solution)/shard_map/hand_out/pallas_call | solution.py:530

commit v6 on v5

--- a/solution.py
+++ b/solution.py
@@ -14,6 +14,7 @@
 HI = lax.Precision.HIGHEST
 
 TOK = 128
+PIECES = 16
 NZ, NY = 8, 4
 HEADS = 16
 QW = 256
@@ -160,7 +161,7 @@
         part = kv.at[core, slot, 0]
         hand_own.append(plan(part, part, kvh_s.at[7 + slot], kvh_r.at[7 + slot], partner, z >= slot, z >= slot))
     z_chain = [
-        plan(rz.at[i], rin.at[i], z_s.at[i], z_r.at[i], next_row, z < NZ - 1, z > 0) for i in range(NZ)
+        plan(rz.at[i], rin.at[i], z_s.at[i], z_r.at[i], next_row, z < NZ - 1, z > 0) for i in range(PIECES)
     ]
     y_out = [
         plan(gout.at[j], fs.at[y], y_s.at[4, j], y_r.at[4, y], (z * NY + j, head), y != j) for j in range(NY)
@@ -341,7 +342,7 @@
         state = own if state is None else state * jnp.exp(logs[j]) + own
         if j < NY - 1:
             prior[j + 1] = state.astype(BF)
-    change[...] = state.reshape(NZ, 32, QW)
+    change[...] = state.reshape(PIECES, QW // PIECES, QW)
     pump(3, [0])
     hand_own[4].start()
 
@@ -386,7 +387,7 @@
         copy.wait_recv()
     pl.when(late)(attend_column)
     pl.when(late)(attend_own)
-    for i in range(NZ):
+    for i in range(PIECES):
         z_chain[i].wait_recv()
         rz[i] = (rin[i].astype(F32) * row_decay + change[i]).astype(BF)
         z_chain[i].start()
@@ -485,10 +486,10 @@
             pltpu.VMEM((NY, TOK, QW), BF),
             pltpu.VMEM((NY, 8, TOK), F32),
             pltpu.VMEM((NY, 8, TOK), F32),
-            pltpu.VMEM((NZ, 32, QW), F32),
+            pltpu.VMEM((PIECES, QW // PIECES, QW), F32),
             pltpu.VMEM((NY, QW, QW), BF),
-            pltpu.VMEM((NZ, 32, QW), BF),
-            pltpu.VMEM((NZ, 32, QW), BF),
+            pltpu.VMEM((PIECES, QW // PIECES, QW), BF),
+            pltpu.VMEM((PIECES, QW // PIECES, QW), BF),
             pltpu.VMEM((NY, TOK, QW), F32),
             pltpu.VMEM((NY, TOK, QW), BF),
             pltpu.VMEM((NY, TOK, QW), BF),
@@ -506,8 +507,8 @@
             dma((11,)),
             dma((5, NY)),
             dma((5, NY)),
-            dma((NZ,)),
-            dma((NZ,)),
+            dma((PIECES,)),
+            dma((PIECES,)),
             dma((NY,)),
             dma((NY,)),
             dma((4, NY)),

time: 49.7 us -> 49.6 us (level)
  the two profiles are of different devices: /device:TPU:505 before, /device:TPU:455 now
where the time goes in v6:
time: 49.6 us; the launch traced here: 49.4 us
  Pallas kernels  48.7 us (98%)
  between operations  0.64 us (1%)
    pallas_call x1, Pallas kernels, shards(): pl.pallas_call(kernel, out_shape=(jax.ShapeDtypeStruct((TOK, 1024), BF),...  47 us
    pallas_call x1, Pallas kernels, shards(): pl.pallas_call(hand_out, out_shape=(jax.ShapeDtypeStruct((TOK, 1024), BF)...  1.74 us

profile of v6, /device:TPU:455, one launch (start us, length us, event | category | flops | bytes accessed | tf_op | source)
XLA Modules:
  0.0 49.4 jit_solution(3400386891539337705)
XLA Ops:
  0.6 47.0 %hybrid_mixer.1 = (bf16[128,1024]{1,0:T(8,128)(2,1)}, bf16[128,512]{1,0:T(8,128)(2,1)}) custom-call(bf16[128,1024]{1,0:T(8,128)(2,1)} %x_hbm.1, bf16[128,1024]{1,0:T(8,128)(2,1)} %gate_hbm.1, f32[16,128]{1,0:T(8,128)} %bitcast.8, f32[16,128]{1,0:T(8,128)} %bitcast.9, bf16[128,128]{1,0:T(8,128)(2,1)} %b_hbm.1, bf16[128,128]{1,0:T(8,128)(2,1)} %c_hbm.1, ...), custom_call_target="tpu_custom_call" | custom-call | tf_op jit(solution)/shard_map/hybrid_mixer/pallas_call | solution.py:468
  47.6 1.7 %hand_out.1 = (bf16[128,1024]{1,0:T(8,128)(2,1)}, bf16[128,512]{1,0:T(8,128)(2,1)}) custom-call(bf16[128,1024]{1,0:T(8,128)(2,1)} %get-tuple-element.4.ssm, bf16[128,512]{1,0:T(8,128)(2,1)} %get-tuple-element.5.attention), custom_call_target="tpu_custom_call" | custom-call | tf_op jit(solution)/shard_map/hand_out/pallas_call | solution.py:531
